TPU v7x, 1024 devices: a whole 4x8x16 slice. The times are simulated.
1024 devices in a mesh: blk: 256 (over y, z, core), sub: 4 (over x).
Axes of the slice: x: 4, y: 8, z: 16, core: 2. Of those that a mesh axis runs over, the one named last changes fastest.
Arguments:
- correlation: float32 [2048, 6, 128, 128], P(('blk', 'sub')), may hold values from -3 to 3, as said below
- factor: float32 [2048, 6, 128, 128], P(('blk', 'sub')), may hold values from -2 to 2, as said below
- pattern: int32 [2048, 6], replicated, may hold values from 0 to 2047, as said below
Outputs:
- refined: float32 [2048, 6, 128, 128], P(('blk', 'sub'))
- correction: float32 [2048, 6, 128, 128], P(('blk', 'sub'))
Inputs may be any that keep to these rules, and one draw needn't show every extreme that they name: `pattern`: slot 0 of tile row i is i itself; the other 5 slots name all but one of the tile rows i - 3 to i + 3 other than i, taken modulo 2048, in increasing offset. `correlation`: slot 0 of each tile row holds the diagonal tile. `factor`: slot 0 of each tile row holds the diagonal tile.
All inputs are finite; a program needn't handle non-finite values.
Results may differ from a plain program's by a relative error of at most 0.0003.
Values sent between devices are 32-bit elements; how exact they have to be, the bound alone decides.
A program may use at most 64 MiB of HBM per device.

v0:
```python
import jax
import jax.numpy as jnp
from jax import lax
from jax.sharding import PartitionSpec as P

REACH = 3


def passed_along(value, axis, by):
    size = lax.axis_size(axis)
    return lax.ppermute(value, axis, [(i, (i + by) % size) for i in range(size)])


def select_tiles(window_flat, pattern, start_row, rows_wanted, columns_wanted):
    total_rows = pattern.shape[0]
    width_slots = pattern.shape[1]
    zero_index = window_flat.shape[0] - 1
    window_pos = (rows_wanted - start_row + REACH) % total_rows
    matches = pattern[rows_wanted] == columns_wanted[..., None]
    slot_index = jnp.argmax(matches, axis=-1)
    present = jnp.any(matches, axis=-1)
    flat_index = jnp.where(present, window_pos * width_slots + slot_index, zero_index)
    return window_flat[flat_index]


def neighbour_window(tiles):
    rows_here = tiles.shape[0]
    tile_size = tiles.shape[2]
    edge_count = REACH - rows_here
    nearby = [passed_along(tiles, ("blk", "sub"), offset) for offset in (1, -1)]
    sources = ((2, tiles[rows_here - edge_count :]), (-2, tiles[:edge_count]))
    further = [passed_along(source, ("blk", "sub"), offset) for offset, source in sources]
    pieces = [further[0], nearby[0], tiles, nearby[1], further[1]]
    flat_pieces = [piece.reshape((-1, tile_size, tile_size)) for piece in pieces]
    flat_pieces.append(jnp.zeros((1, tile_size, tile_size), tiles.dtype))
    return jnp.concatenate(flat_pieces, axis=0)


def body(correlation, factor, pattern):
    rows_here = correlation.shape[0]
    start_row = lax.axis_index(("blk", "sub")) * rows_here
    total_rows = pattern.shape[0]
    local_rows = start_row + jnp.arange(rows_here, dtype=jnp.int32)
    own_cols = lax.dynamic_slice_in_dim(pattern, start_row, rows_here, 0)
    width_slots = own_cols.shape[1]
    grid_shape = (rows_here, width_slots, width_slots)
    column_rows = jnp.broadcast_to(own_cols[:, None, :], grid_shape)
    column_want = jnp.broadcast_to(own_cols[:, :, None], grid_shape)
    offsets = jnp.arange(-REACH, REACH + 1, dtype=jnp.int32)
    candidates = (local_rows[:, None] + offsets[None, :]) % total_rows
    candidate_shape = (rows_here, width_slots, offsets.shape[0])
    candidate_rows = jnp.broadcast_to(candidates[:, None, :], candidate_shape)
    candidate_want = jnp.broadcast_to(own_cols[:, :, None], candidate_shape)
    diagonal_want = jnp.broadcast_to(local_rows[:, None], candidates.shape)
    identity = jnp.eye(correlation.shape[2], dtype=jnp.float32)
    factor_window = neighbour_window(factor)
    chosen = select_tiles(factor_window, pattern, start_row, column_rows, column_want)
    product = jnp.einsum("tqab,tpqbc->tpac", correlation, chosen, precision=lax.Precision.HIGHEST)
    product_window = neighbour_window(product)
    left_side = select_tiles(factor_window, pattern, start_row, candidates, diagonal_want)
    right_side = select_tiles(product_window, pattern, start_row, candidate_rows, candidate_want)
    gram_tiles = jnp.einsum(
        "toba,tpobc->tpac", left_side, right_side, precision=lax.Precision.HIGHEST
    )
    correction = (-gram_tiles).at[:, 0].add(identity)
    correction_window = neighbour_window(correction)
    picked = select_tiles(correction_window, pattern, start_row, column_rows, column_want)
    update = jnp.einsum("tqab,tpqbc->tpac", factor, picked, precision=lax.Precision.HIGHEST)
    factor = factor + 0.5 * update
    return (factor, correction)


def solution(mesh):
    in_specs = (P(("blk", "sub"), None, None, None), P(("blk", "sub"), None, None, None), P())
    out_specs = (P(("blk", "sub"), None, None, None), P(("blk", "sub"), None, None, None))
    return jax.shard_map(body, mesh=mesh, in_specs=in_specs, out_specs=out_specs, check_vma=False)
```

profile of v0, /device:TPU:1, one launch (start us, length us, event | category | flops | bytes accessed | tf_op | source)
XLA Modules:
  0.0 195.3 jit_solution(14589257358842959105)
XLA Ops:
  0.7 5.9 %collective-permute-start.2 = (f32[2,6,128,128]{3,2,1,0:T(8,128)}, f32[2,6,128,128]{3,2,1,0:T(8,128)S(1)}, u32[]{:S(2)}, u32[]{:S(2)}) collective-permute-start(f32[2,6,128,128]{3,2,1,0:T(8,128)} %param.6), channel_id=1, source_target_pairs={{0,1023},{1,0},{2,1},{3,2},{4,3},{5,4},{6,5},{7,6},{8,7},{9,8},{10... | collective-permute-start | bytes 2359304 | tf_op jit(solution)/shard_map/ppermute | solution.py:11
  6.6 1.9 collective-permute-start.1
  8.5 2.0 %fusion.19 = (f32[1,6,128,128]{3,2,1,0:T(8,128)}, f32[1,6,128,128]{3,2,1,0:T(8,128)}) fusion(f32[2,6,128,128]{3,2,1,0:T(8,128)} %param.6), kind=kLoop, calls=%fused_computation.89 | loop fusion | bytes 1572864 | tf_op jit(solution)/shard_map/slice | solution.py:31
  10.5 4.2 %collective-permute-start.3 = (f32[1,6,128,128]{3,2,1,0:T(8,128)}, f32[1,6,128,128]{3,2,1,0:T(8,128)}, u32[]{:S(2)}, u32[]{:S(2)}) collective-permute-start(f32[1,6,128,128]{3,2,1,0:T(8,128)} %get-tuple-element.39), channel_id=1, source_target_pairs={{0,1022},{1,1023},{2,0},{3,1},{4,2},{5,3},{6,4},{7,5},{8,6},{9,7},... | collective-permute-start | bytes 1179656 | tf_op jit(solution)/shard_map/ppermute | solution.py:11
  14.7 2.6 %collective-permute-start = (f32[1,6,128,128]{3,2,1,0:T(8,128)}, f32[1,6,128,128]{3,2,1,0:T(8,128)}, u32[]{:S(2)}, u32[]{:S(2)}) collective-permute-start(f32[1,6,128,128]{3,2,1,0:T(8,128)} %get-tuple-element.40), channel_id=1, source_target_pairs={{0,2},{1,3},{2,4},{3,5},{4,6},{5,7},{6,8},{7,9},{8,10},{9,11},{10,... | collective-permute-start | bytes 1179656 | tf_op jit(solution)/shard_map/ppermute | solution.py:11
  17.5 0.8 compare_and_fusion
  18.3 0.1 copy.25
  18.4 0.1 copy.31
  18.5 1.2 copy.26
  19.8 0.1 copy.29
  19.9 0.1 copy.23
  20.0 0.1 copy.30
  20.1 0.1 copy.24
  20.3 0.6 gather_fusion.4
  20.9 0.1 copy.37
  21.1 0.6 iota_reduce_fusion.2
  21.9 0.6 gather_fusion
  22.5 0.6 gather_fusion.2
  23.3 0.1 reshape.232
  23.5 0.6 iota_reduce_fusion.1
  24.4 0.6 iota_reduce_fusion
  25.0 31.1 %collective-permute-done = f32[1,6,128,128]{3,2,1,0:T(8,128)} collective-permute-done((f32[1,6,128,128]{3,2,1,0:T(8,128)}, f32[1,6,128,128]{3,2,1,0:T(8,128)}, u32[]{:S(2)}, u32[]{:S(2)}) %collective-permute-start) | collective-permute-done | bytes 393248 | tf_op jit(solution)/shard_map/ppermute | solution.py:11
  56.1 1.8 bitcast_dynamic-update-slice_fusion.5
  57.9 2.1 %constant_dynamic-update-slice_fusion.3 = f32[49,128,128]{2,1,0:T(8,128)} fusion(f32[49,128,128]{2,1,0:T(8,128)} %bitcast_dynamic-update-slice_fusion.5, f32[12,128,128]{2,1,0:T(8,128)} %bitcast.1), kind=kLoop, calls=%fused_computation.32 | loop fusion | bytes 1572864
  59.9 1.0 constant_dynamic-update-slice_fusion.2
  60.9 0.9 constant_dynamic-update-slice_fusion.1
  61.8 1.8 bitcast_dynamic-update-slice_fusion.4
  63.6 0.6 constant_dynamic-update-slice_fusion
  64.2 4.9 %gather_fusion.1 = f32[72,128,128]{2,1,0:T(8,128)} fusion(f32[49,128,128]{2,1,0:T(8,128)} %constant_dynamic-update-slice_fusion, s32[1024]{0:T(1024)S(1)} %pad_clamp_fusion.4), kind=kCustom, calls=%fused_computation.1 | custom fusion | bytes 9437472 | tf_op jit(solution)/shard_map/gather | solution.py:23
  69.1 9.4 %fusion.6 = f32[2,6,128,128,1]{3,2,4,1,0:T(8,128)S(1)} fusion(f32[2,6,6,128,128]{4,3,2,1,0:T(8,128)} %bitcast.85, f32[2,6,128,128]{3,2,1,0:T(8,128)S(1)} %copy-done), kind=kOutput, calls=%fused_computation.15 | convolution fusion | flops 1811939328 | bytes 6291456 | tf_op jit(solution)/shard_map/tqab,tpqbc->tpac/dot_general | solution.py:58
  78.5 0.9 fusion.18
  79.4 1.9 collective-permute-start.5
  81.3 1.9 collective-permute-start.4
  83.3 4.8 %collective-permute-start.6 = (f32[2,6,128,128]{2,3,1,0:T(8,128)S(1)}, f32[2,6,128,128]{2,3,1,0:T(8,128)}, u32[]{:S(2)}, u32[]{:S(2)}) collective-permute-start(f32[2,6,128,128]{2,3,1,0:T(8,128)S(1)} %bitcast.90), channel_id=1, source_target_pairs={{0,1023},{1,0},{2,1},{3,2},{4,3},{5,4},{6,5},{7,6},{8,7},{9,8},{10... | collective-permute-start | bytes 2359304 | tf_op jit(solution)/shard_map/ppermute | solution.py:11
  88.3 2.5 %gather_fusion.5 = f32[14,128,128]{2,1,0:T(8,128)S(1)} fusion(f32[49,128,128]{2,1,0:T(8,128)} %constant_dynamic-update-slice_fusion, s32[1024]{0:T(1024)S(1)} %pad_clamp_fusion), kind=kCustom, calls=%fused_computation.5 | custom fusion | bytes 1835064 | tf_op jit(solution)/shard_map/gather | solution.py:23
  90.8 4.8 %collective-permute-start.7 = (f32[1,6,128,128]{2,3,1,0:T(8,128)}, f32[1,6,128,128]{2,3,1,0:T(8,128)S(1)}, u32[]{:S(2)}, u32[]{:S(2)}) collective-permute-start(f32[1,6,128,128]{2,3,1,0:T(8,128)} %get-tuple-element.37), channel_id=1, source_target_pairs={{0,1022},{1,1023},{2,0},{3,1},{4,2},{5,3},{6,4},{7,5},{8,6},{9,7},... | collective-permute-start | bytes 1179656 | tf_op jit(solution)/shard_map/ppermute | solution.py:11
  95.7 13.9 %collective-permute-done.4 = f32[1,6,128,128]{2,3,1,0:T(8,128)} collective-permute-done((f32[1,6,128,128]{2,3,1,0:T(8,128)}, f32[1,6,128,128]{2,3,1,0:T(8,128)}, u32[]{:S(2)}, u32[]{:S(2)}) %collective-permute-start.4) | collective-permute-done | bytes 393248 | tf_op jit(solution)/shard_map/ppermute | solution.py:11
  109.6 1.8 bitcast_dynamic-update-slice_fusion.3
  111.4 7.9 %collective-permute-done.5 = f32[2,6,128,128]{2,3,1,0:T(8,128)} collective-permute-done((f32[2,6,128,128]{2,3,1,0:T(8,128)S(1)}, f32[2,6,128,128]{2,3,1,0:T(8,128)}, u32[]{:S(2)}, u32[]{:S(2)}) %collective-permute-start.5) | collective-permute-done | bytes 786464 | tf_op jit(solution)/shard_map/ppermute | solution.py:11
  119.3 2.1 %constant_dynamic-update-slice_fusion.7 = f32[49,128,128]{1,2,0:T(8,128)} fusion(f32[49,128,128]{1,2,0:T(8,128)} %bitcast_dynamic-update-slice_fusion.3, f32[12,128,128]{1,2,0:T(8,128)} %bitcast.13), kind=kLoop, calls=%fused_computation.36 | loop fusion | bytes 1572864
  121.4 0.9 constant_dynamic-update-slice_fusion.6
  122.3 2.1 %constant_dynamic-update-slice_fusion.5 = f32[49,128,128]{1,2,0:T(8,128)} fusion(f32[49,128,128]{1,2,0:T(8,128)} %constant_dynamic-update-slice_fusion.6, f32[12,128,128]{1,2,0:T(8,128)} %bitcast.15), kind=kLoop, calls=%fused_computation.34 | loop fusion | bytes 1572864
  124.4 0.8 bitcast_dynamic-update-slice_fusion.2
  125.2 0.6 constant_dynamic-update-slice_fusion.4
  125.8 5.2 %gather_fusion.3 = f32[84,128,128]{1,2,0:T(8,128)} fusion(f32[49,128,128]{1,2,0:T(8,128)} %constant_dynamic-update-slice_fusion.4, s32[1024]{0:T(1024)S(1)} %pad_clamp_fusion.2), kind=kCustom, calls=%fused_computation.3 | custom fusion | bytes 11010384 | tf_op jit(solution)/shard_map/gather | solution.py:23
  131.0 6.5 %fusion.4 = f32[2,6,128,128]{2,3,1,0:T(8,128)S(1)} fusion(f32[2,6,7,128,128]{3,4,2,1,0:T(8,128)} %bitcast.83, f32[2,7,128,128,1]{3,2,1,4,0:T(8,128)S(1)} %bitcast.92), kind=kOutput, calls=%fused_computation.13 | convolution fusion | flops 2114125824 | bytes 7208960 | tf_op jit(solution)/shard_map/toba,tpobc->tpac/dot_general | solution.py:62
  137.6 1.9 collective-permute-start.9
  139.5 0.9 fusion.17
  140.4 1.9 collective-permute-start.8
  142.3 4.9 %collective-permute-start.10 = (f32[2,6,128,128]{2,3,1,0:T(8,128)S(1)}, f32[2,6,128,128]{2,3,1,0:T(8,128)}, u32[]{:S(2)}, u32[]{:S(2)}) collective-permute-start(f32[2,6,128,128]{2,3,1,0:T(8,128)S(1)} %fusion.8), channel_id=1, source_target_pairs={{0,1023},{1,0},{2,1},{3,2},{4,3},{5,4},{6,5},{7,6},{8,7},{9,8},{10... | collective-permute-start | bytes 2359304 | tf_op jit(solution)/shard_map/ppermute | solution.py:11
  147.2 0.3 copy.38
  147.5 1.1 copy.40
  148.6 5.0 %collective-permute-start.11 = (f32[1,6,128,128]{2,3,1,0:T(8,128)}, f32[1,6,128,128]{2,3,1,0:T(8,128)S(1)}, u32[]{:S(2)}, u32[]{:S(2)}) collective-permute-start(f32[1,6,128,128]{2,3,1,0:T(8,128)} %get-tuple-element.35), channel_id=1, source_target_pairs={{0,1022},{1,1023},{2,0},{3,1},{4,2},{5,3},{6,4},{7,5},{8,6},{9,7},... | collective-permute-start | bytes 1179656 | tf_op jit(solution)/shard_map/ppermute | solution.py:11
  153.6 12.2 %collective-permute-done.8 = f32[1,6,128,128]{2,3,1,0:T(8,128)S(1)} collective-permute-done((f32[1,6,128,128]{2,3,1,0:T(8,128)}, f32[1,6,128,128]{2,3,1,0:T(8,128)S(1)}, u32[]{:S(2)}, u32[]{:S(2)}) %collective-permute-start.8) | collective-permute-done | bytes 393248 | tf_op jit(solution)/shard_map/ppermute | solution.py:11
  165.8 0.8 bitcast_dynamic-update-slice_fusion.1
  166.6 10.5 %collective-permute-done.9 = f32[2,6,128,128]{2,3,1,0:T(8,128)} collective-permute-done((f32[2,6,128,128]{2,3,1,0:T(8,128)S(1)}, f32[2,6,128,128]{2,3,1,0:T(8,128)}, u32[]{:S(2)}, u32[]{:S(2)}) %collective-permute-start.9) | collective-permute-done | bytes 786464 | tf_op jit(solution)/shard_map/ppermute | solution.py:11
  177.1 2.1 %constant_dynamic-update-slice_fusion.11 = f32[49,128,128]{1,2,0:T(8,128)} fusion(f32[49,128,128]{1,2,0:T(8,128)} %bitcast_dynamic-update-slice_fusion.1, f32[12,128,128]{1,2,0:T(8,128)} %bitcast.25), kind=kLoop, calls=%fused_computation.40 | loop fusion | bytes 1572864
  179.2 1.0 constant_dynamic-update-slice_fusion.10
  180.1 2.1 %constant_dynamic-update-slice_fusion.9 = f32[49,128,128]{1,2,0:T(8,128)} fusion(f32[49,128,128]{1,2,0:T(8,128)} %constant_dynamic-update-slice_fusion.10, f32[12,128,128]{1,2,0:T(8,128)} %bitcast.27), kind=kLoop, calls=%fused_computation.38 | loop fusion | bytes 1572864
  182.2 0.8 bitcast_dynamic-update-slice_fusion
  183.0 0.6 constant_dynamic-update-slice_fusion.8
  183.6 4.9 %gather_fusion.6 = f32[72,128,128]{1,2,0:T(8,128)} fusion(f32[49,128,128]{1,2,0:T(8,128)} %constant_dynamic-update-slice_fusion.8, s32[1024]{0:T(1024)S(1)} %pad_clamp_fusion.4), kind=kCustom, calls=%fused_computation.6 | custom fusion | bytes 9437472 | tf_op jit(solution)/shard_map/gather | solution.py:23
  188.5 5.7 %fusion.2 = f32[2,6,128,128]{2,3,1,0:T(8,128)S(1)} fusion(f32[2,6,128,128]{2,3,1,0:T(8,128)S(1)} %copy.38, f32[2,6,6,128,128]{3,4,2,1,0:T(8,128)} %bitcast.84, f32[2,6,128,128]{3,2,1,0:T(8,128)S(1)} %copy-done.1), kind=kOutput, calls=%fused_computation.10 | convolution fusion | flops 1812332544 | bytes 7077888 | tf_op jit(solution)/shard_map/tqab,tpqbc->tpac/dot_general | solution.py:68
  194.2 1.1 copy.39
  (45 shorter events, 1.5 us)
Async XLA Ops:
  0.6 68.5 %copy-start = (f32[2,6,128,128]{3,2,1,0:T(8,128)S(1)}, f32[2,6,128,128]{3,2,1,0:T(8,128)}, u32[]{:S(2)}) copy-start(f32[2,6,128,128]{3,2,1,0:T(8,128)} %param.5) | copy-start | bytes 2359300
  0.6 59.3 %copy-start.1 = (f32[2,6,128,128]{3,2,1,0:T(8,128)S(1)}, f32[2,6,128,128]{3,2,1,0:T(8,128)}, u32[]{:S(2)}) copy-start(f32[2,6,128,128]{3,2,1,0:T(8,128)} %param.6) | copy-start | bytes 2359300
  0.7 60.2 %collective-permute-start.2 = (f32[2,6,128,128]{3,2,1,0:T(8,128)}, f32[2,6,128,128]{3,2,1,0:T(8,128)S(1)}, u32[]{:S(2)}, u32[]{:S(2)}) collective-permute-start(f32[2,6,128,128]{3,2,1,0:T(8,128)} %param.6), channel_id=1, source_target_pairs={{0,1023},{1,0},{2,1},{3,2},{4,3},{5,4},{6,5},{7,6},{8,7},{9,8},{10... | collective-permute-start | bytes 2359304 | tf_op jit(solution)/shard_map/ppermute | solution.py:11
  6.6 51.3 %collective-permute-start.1 = (f32[2,6,128,128]{3,2,1,0:T(8,128)}, f32[2,6,128,128]{3,2,1,0:T(8,128)}, u32[]{:S(2)}, u32[]{:S(2)}) collective-permute-start(f32[2,6,128,128]{3,2,1,0:T(8,128)} %param.6), channel_id=1, source_target_pairs={{0,1},{1,2},{2,3},{3,4},{4,5},{5,6},{6,7},{7,8},{8,9},{9,10},{10,1... | collective-permute-start | bytes 2359304 | tf_op jit(solution)/shard_map/ppermute | solution.py:11
  10.5 51.3 %collective-permute-start.3 = (f32[1,6,128,128]{3,2,1,0:T(8,128)}, f32[1,6,128,128]{3,2,1,0:T(8,128)}, u32[]{:S(2)}, u32[]{:S(2)}) collective-permute-start(f32[1,6,128,128]{3,2,1,0:T(8,128)} %get-tuple-element.39), channel_id=1, source_target_pairs={{0,1022},{1,1023},{2,0},{3,1},{4,2},{5,3},{6,4},{7,5},{8,6},{9,7},... | collective-permute-start | bytes 1179656 | tf_op jit(solution)/shard_map/ppermute | solution.py:11
  14.7 41.3 %collective-permute-start = (f32[1,6,128,128]{3,2,1,0:T(8,128)}, f32[1,6,128,128]{3,2,1,0:T(8,128)}, u32[]{:S(2)}, u32[]{:S(2)}) collective-permute-start(f32[1,6,128,128]{3,2,1,0:T(8,128)} %get-tuple-element.40), channel_id=1, source_target_pairs={{0,2},{1,3},{2,4},{3,5},{4,6},{5,7},{6,8},{7,9},{8,10},{9,11},{10,... | collective-permute-start | bytes 1179656 | tf_op jit(solution)/shard_map/ppermute | solution.py:11
  79.4 39.9 %collective-permute-start.5 = (f32[2,6,128,128]{2,3,1,0:T(8,128)S(1)}, f32[2,6,128,128]{2,3,1,0:T(8,128)}, u32[]{:S(2)}, u32[]{:S(2)}) collective-permute-start(f32[2,6,128,128]{2,3,1,0:T(8,128)S(1)} %bitcast.89), channel_id=1, source_target_pairs={{0,1},{1,2},{2,3},{3,4},{4,5},{5,6},{6,7},{7,8},{8,9},{9,10},{10,1... | collective-permute-start | bytes 2359304 | tf_op jit(solution)/shard_map/ppermute | solution.py:11
  81.3 28.3 %collective-permute-start.4 = (f32[1,6,128,128]{2,3,1,0:T(8,128)}, f32[1,6,128,128]{2,3,1,0:T(8,128)}, u32[]{:S(2)}, u32[]{:S(2)}) collective-permute-start(f32[1,6,128,128]{2,3,1,0:T(8,128)} %get-tuple-element.38), channel_id=1, source_target_pairs={{0,2},{1,3},{2,4},{3,5},{4,6},{5,7},{6,8},{7,9},{8,10},{9,11},{10,... | collective-permute-start | bytes 1179656 | tf_op jit(solution)/shard_map/ppermute | solution.py:11
  83.3 39.0 %collective-permute-start.6 = (f32[2,6,128,128]{2,3,1,0:T(8,128)S(1)}, f32[2,6,128,128]{2,3,1,0:T(8,128)}, u32[]{:S(2)}, u32[]{:S(2)}) collective-permute-start(f32[2,6,128,128]{2,3,1,0:T(8,128)S(1)} %bitcast.90), channel_id=1, source_target_pairs={{0,1023},{1,0},{2,1},{3,2},{4,3},{5,4},{6,5},{7,6},{8,7},{9,8},{10... | collective-permute-start | bytes 2359304 | tf_op jit(solution)/shard_map/ppermute | solution.py:11
  90.8 33.5 %collective-permute-start.7 = (f32[1,6,128,128]{2,3,1,0:T(8,128)}, f32[1,6,128,128]{2,3,1,0:T(8,128)S(1)}, u32[]{:S(2)}, u32[]{:S(2)}) collective-permute-start(f32[1,6,128,128]{2,3,1,0:T(8,128)} %get-tuple-element.37), channel_id=1, source_target_pairs={{0,1022},{1,1023},{2,0},{3,1},{4,2},{5,3},{6,4},{7,5},{8,6},{9,7},... | collective-permute-start | bytes 1179656 | tf_op jit(solution)/shard_map/ppermute | solution.py:11
  137.6 39.5 %collective-permute-start.9 = (f32[2,6,128,128]{2,3,1,0:T(8,128)S(1)}, f32[2,6,128,128]{2,3,1,0:T(8,128)}, u32[]{:S(2)}, u32[]{:S(2)}) collective-permute-start(f32[2,6,128,128]{2,3,1,0:T(8,128)S(1)} %fusion.8), channel_id=1, source_target_pairs={{0,1},{1,2},{2,3},{3,4},{4,5},{5,6},{6,7},{7,8},{8,9},{9,10},{10,1... | collective-permute-start | bytes 2359304 | tf_op jit(solution)/shard_map/ppermute | solution.py:11
  140.4 25.4 %collective-permute-start.8 = (f32[1,6,128,128]{2,3,1,0:T(8,128)}, f32[1,6,128,128]{2,3,1,0:T(8,128)S(1)}, u32[]{:S(2)}, u32[]{:S(2)}) collective-permute-start(f32[1,6,128,128]{2,3,1,0:T(8,128)} %get-tuple-element.36), channel_id=1, source_target_pairs={{0,2},{1,3},{2,4},{3,5},{4,6},{5,7},{6,8},{7,9},{8,10},{9,11},{10,... | collective-permute-start | bytes 1179656 | tf_op jit(solution)/shard_map/ppermute | solution.py:11
  142.3 37.8 %collective-permute-start.10 = (f32[2,6,128,128]{2,3,1,0:T(8,128)S(1)}, f32[2,6,128,128]{2,3,1,0:T(8,128)}, u32[]{:S(2)}, u32[]{:S(2)}) collective-permute-start(f32[2,6,128,128]{2,3,1,0:T(8,128)S(1)} %fusion.8), channel_id=1, source_target_pairs={{0,1023},{1,0},{2,1},{3,2},{4,3},{5,4},{6,5},{7,6},{8,7},{9,8},{10... | collective-permute-start | bytes 2359304 | tf_op jit(solution)/shard_map/ppermute | solution.py:11
  148.6 33.6 %collective-permute-start.11 = (f32[1,6,128,128]{2,3,1,0:T(8,128)}, f32[1,6,128,128]{2,3,1,0:T(8,128)S(1)}, u32[]{:S(2)}, u32[]{:S(2)}) collective-permute-start(f32[1,6,128,128]{2,3,1,0:T(8,128)} %get-tuple-element.35), channel_id=1, source_target_pairs={{0,1022},{1,1023},{2,0},{3,1},{4,2},{5,3},{6,4},{7,5},{8,6},{9,7},... | collective-permute-start | bytes 1179656 | tf_op jit(solution)/shard_map/ppermute | solution.py:11
where the time goes:
time: 196 us; the launch traced here: 195 us
  waiting for transfers between devices  75.6 us (39%)
  local copies, waits for them, and re-layouts  52.2 us (27%)
  starting transfers between devices  41.8 us (21%)
  matrix products  21.5 us (11%)
  other arithmetic  3.23 us (2%)
    ppermute x12, waiting for transfers between devices, passed_along(): lax.ppermute(value, axis, [(i, (i + by) % size) for i in range(size)])  75.6 us
    ppermute x12, starting transfers between devices, passed_along(): lax.ppermute(value, axis, [(i, (i + by) % size) for i in range(size)])  41.8 us
    unnamed x23, local copies, waits for them, and re-layouts  25.7 us
    gather x4, local copies, waits for them, and re-layouts, select_tiles(): return window_flat[flat_index]  17.5 us
    dot_general x1, matrix products, body(): jnp.einsum('tqab,tpqbc->tpac', correlation, chosen, precision=lax.Precisi...  9.35 us
    dot_general x1, matrix products, body(): jnp.einsum('toba,tpobc->tpac', left_side, right_side, precision=lax.Preci...  6.49 us
    dot_general x1, matrix products, body(): jnp.einsum('tqab,tpqbc->tpac', factor, picked, precision=lax.Precision.HI...  5.69 us
  transfers between devices with their start and end apart: 12, of which 5 were waited for; matrix products, arithmetic and copies ran while one was open for 17% of the time, Pallas kernels for 0%

commit v1 on v0

v1 whole, which is shorter than its diff:
```python
import jax
import jax.numpy as jnp
from jax import lax
from jax.experimental import pallas as pl
from jax.experimental.pallas import tpu as pltpu
from jax.sharding import PartitionSpec as P

T = 128
SLOTS = 6
OFFS = (-3, -2, -1, 1, 2, 3)
F32 = jnp.float32
BF16 = jnp.bfloat16
MESH = pl.DeviceIdType.MESH


def halves(x):
    hi = x.astype(BF16)
    return hi, (x - hi.astype(F32)).astype(BF16)


def dot(a, b):
    return jnp.dot(a, b, preferred_element_type=F32)


def kernel(
    corr_hbm, fact_hbm, pat_hbm, refined_hbm, correction_hbm,
    pat, zraw, sraw, zwin, scat, zh, zl, zth, ztl, psend, pcol, pcat,
    dsend, drow, dcat, usend, urow, dout, uout, lsem, ssem, rsem,
):
    blks, subs = lax.axis_size("blk"), lax.axis_size("sub")
    world = blks * subs
    rows_all = 2 * world
    me = lax.axis_index("blk") * subs + lax.axis_index("sub")

    def device(by):
        d = lax.rem(me + by + world, world)
        return (lax.div(d, subs), lax.rem(d, subs))

    def row_of(w):
        return lax.rem(2 * me + (w - 3) + rows_all, rows_all)

    load_pat = pltpu.make_async_copy(pat_hbm, pat, lsem.at[0])
    load_z = pltpu.make_async_copy(fact_hbm, zraw.at[:, pl.ds(0, SLOTS)], lsem.at[1])
    load_s = pltpu.make_async_copy(corr_hbm, sraw.at[:, pl.ds(0, SLOTS)], lsem.at[2])
    load_z.start()
    load_pat.start()
    load_s.start()

    barrier = pltpu.get_barrier_semaphore()
    for by in (-2, -1, 1, 2):
        pl.semaphore_signal(barrier, inc=1, device_id=device(by), device_id_type=MESH)

    zero = jnp.zeros((T, T), F32)
    for r in range(2):
        zraw[r, SLOTS] = zero
        sraw[r, SLOTS] = zero
    zero16 = jnp.zeros((T, T), BF16)
    for a in range(8):
        for b in range(8):
            if abs(a - b) > 3:
                for ref in (zh, zl, zth, ztl):
                    ref[a * T : (a + 1) * T, b * T : (b + 1) * T] = zero16
    for base in (0, 2 * T):
        scat[base : base + T, 7 * T :] = zero16
        scat[base + T : base + 2 * T, :T] = zero16

    load_pat.wait()
    low = []
    for r in range(2):
        row = row_of(3 + r)
        low.append([None] + [
            (pat[s, row] == row_of(3 + r + OFFS[s - 1])).astype(jnp.int32) for s in range(1, SLOTS)
        ])

    def slot_of(r, p):
        here = jnp.int32(SLOTS) if p == 0 else p + low[r][p] * (SLOTS - p)
        return here if p == 5 else jnp.where(low[r][p + 1] == 1, p + 1, here)

    def present(w, column):
        p = OFFS.index(column - w) if column != w else None
        if p is None:
            return None
        row, want = row_of(w), row_of(column)
        found = jnp.int32(0)
        if p <= 4:
            found = found | (pat[p + 1, row] == want).astype(jnp.int32)
        if p >= 1:
            found = found | (pat[p, row] == want).astype(jnp.int32)
        return found.astype(F32)

    def masked(x, w, column):
        if abs(w - column) > 3:
            return jnp.zeros_like(x)
        m = present(w, column)
        return x if m is None else x * m

    slots = [[slot_of(r, p) for p in range(6)] for r in range(2)]

    def dense(ref, r, o):
        if o == 3:
            return ref[r, 0]
        return ref[r, slots[r][o if o < 3 else o - 1]]

    load_z.wait()
    for r in range(2):
        for o in range(7):
            zwin[3 + r, o] = dense(zraw, r, o)

    pl.semaphore_wait(barrier, 4)

    count = [0]
    started = []

    def send(src, dst, by):
        k = count[0]
        count[0] += 1
        cp = pltpu.make_async_remote_copy(
            src_ref=src, dst_ref=dst, send_sem=ssem.at[k], recv_sem=rsem.at[k],
            device_id=device(by), device_id_type=MESH,
        )
        cp.start()
        started.append(cp)
        return cp

    def send_z(row_from, row_to, o, n, by):
        return send(zwin.at[row_from, pl.ds(o, n)], zwin.at[row_to, pl.ds(o, n)], by)

    r1 = send_z(4, 2, 3, 4, 1)
    l1 = send_z(3, 5, 0, 4, -1)
    r2 = send_z(4, 2, 1, 2, 1)
    l2 = send_z(3, 5, 4, 2, -1)
    r3 = send_z(3, 1, 2, 3, 1)
    l3 = send_z(4, 6, 2, 3, -1)

    def place(w, offsets):
        for o in offsets:
            t = zwin[w, o]
            c = w + o - 3
            hi, lo = halves(t)
            here = (slice(w * T, (w + 1) * T), slice(c * T, (c + 1) * T))
            zh[here] = hi
            zl[here] = lo
            hi, lo = halves(t.T)
            there = here[::-1]
            zth[there] = hi
            ztl[there] = lo

    for r in range(2):
        place(3 + r, range(7))
    load_s.wait()
    for r in range(2):
        for o in range(7):
            hi, lo = halves(dense(sraw, r, o))
            c = r + o
            scat[r * T : (r + 1) * T, c * T : (c + 1) * T] = hi
            scat[(2 + r) * T : (3 + r) * T, c * T : (c + 1) * T] = lo

    r1.wait_recv()
    f1 = send_z(2, 0, 3, 3, 1)
    l1.wait_recv()
    g1 = send_z(5, 7, 1, 3, -1)
    r4 = send_z(3, 1, 5, 2, 1)
    l4 = send_z(4, 6, 0, 2, -1)
    f2 = send_z(2, 0, 6, 1, 1)
    g2 = send_z(5, 7, 0, 1, -1)
    place(2, range(3, 7))
    place(5, range(4))
    r2.wait_recv()
    place(2, range(1, 3))
    l2.wait_recv()
    place(5, range(4, 6))
    r3.wait_recv()
    place(1, range(2, 5))
    l3.wait_recv()
    place(6, range(2, 5))

    def product(rows, columns):
        k, n = slice(rows[0] * T, rows[1] * T), slice(columns[0] * T, columns[1] * T)
        both = dot(scat[:, k], zh[k, n])
        return both[: 2 * T] + both[2 * T :] + dot(scat[: 2 * T, k], zl[k, n])

    def keep_product(x, first, ref, index):
        for n in range(x.shape[1] // T):
            for r in range(2):
                tile = x[r * T : (r + 1) * T, n * T : (n + 1) * T]
                ref[index(first + n, r)] = masked(tile, 3 + r, first + n)

    f1.wait_recv()
    place(0, range(3, 6))
    keep_product(product((0, 6), (0, 3)), 0, psend, lambda c, r: (c, r))
    pl1 = send(psend.at[1], pcol.at[0, pl.ds(5, 2)], -1)
    g1.wait_recv()
    place(7, range(1, 4))
    keep_product(product((2, 8), (5, 8)), 5, psend, lambda c, r: (c, r))
    pr0 = send(psend.at[7, pl.ds(1, 1)], pcol.at[0, pl.ds(0, 1)], 2)
    pr1 = send(psend.at[5], pcol.at[0, pl.ds(1, 2)], 1)
    pl0 = send(psend.at[0, pl.ds(0, 1)], pcol.at[1, pl.ds(7, 1)], -2)
    pr2 = send(psend.at[6], pcol.at[1, pl.ds(1, 2)], 1)
    pl2 = send(psend.at[2], pcol.at[1, pl.ds(5, 2)], -1)

    r4.wait_recv()
    place(1, range(5, 7))
    l4.wait_recv()
    place(6, range(2))
    f2.wait_recv()
    place(0, (6,))
    g2.wait_recv()
    place(7, (0,))
    keep_product(product((0, 8), (3, 5)), 3, pcol, lambda c, r: (c - 3, 3 + r))

    identity = (
        lax.broadcasted_iota(jnp.int32, (T, T), 0) == lax.broadcasted_iota(jnp.int32, (T, T), 1)
    ).astype(F32)

    def banded(high, low_, cat, c):
        here = slice(c * T, (c + 7) * T)
        wide = dot(high[here, here], cat[c])
        return wide[:, :T] + wide[:, T:] + dot(low_[here, here], cat[c, :, :T])

    def gram(c):
        for n in range(7):
            hi, lo = halves(pcol[c, c + n])
            pcat[c, n * T : (n + 1) * T, :T] = hi
            pcat[c, n * T : (n + 1) * T, T:] = lo
        g = banded(zth, ztl, pcat, c)
        for n in range(7):
            w = c + n
            tile = -g[n * T : (n + 1) * T]
            if w == 3 + c:
                tile = tile + identity
            tile = masked(tile, w, 3 + c)
            dsend[c, w] = tile
            if w in (3, 4):
                drow[3 + c, w - 3] = tile
            hi, lo = halves(tile)
            dcat[c, n * T : (n + 1) * T, :T] = hi
            dcat[c, n * T : (n + 1) * T, T:] = lo

    def send_column(src, dst, c):
        if c == 0:
            far = send(src.at[0, pl.ds(0, 1)], dst.at[7, pl.ds(1, 1)], -2)
        else:
            far = send(src.at[1, pl.ds(7, 1)], dst.at[0, pl.ds(0, 1)], 2)
        return [
            far,
            send(src.at[c, pl.ds(5, 2)], dst.at[1 + c], 1),
            send(src.at[c, pl.ds(1, 2)], dst.at[5 + c], -1),
        ]

    def update(c):
        u = banded(zh, zl, dcat, c)
        for n in range(7):
            w = c + n
            tile = u[n * T : (n + 1) * T]
            usend[c, w] = tile
            if w in (3, 4):
                urow[3 + c, w - 3] = tile

    for cp in (pl1, pr0, pr1):
        cp.wait_recv()
    gram(0)
    dcps = send_column(dsend, drow, 0)
    for cp in (pl0, pr2, pl2):
        cp.wait_recv()
    gram(1)
    dcps += send_column(dsend, drow, 1)
    update(0)
    ucps = send_column(usend, urow, 0)
    update(1)
    ucps += send_column(usend, urow, 1)

    def column_of(r, s):
        if s == 0:
            return 3 + r
        position = s - low[r][s]
        return r + position + (position >= 3).astype(jnp.int32)

    for cp in dcps:
        cp.wait_recv()
    for r in range(2):
        for s in range(SLOTS):
            dout[r, s] = drow[column_of(r, s), r]
    keep_d = pltpu.make_async_copy(dout, correction_hbm, lsem.at[3])
    keep_d.start()
    for cp in ucps:
        cp.wait_recv()
    for r in range(2):
        for s in range(SLOTS):
            uout[r, s] = zraw[r, s] + 0.5 * urow[column_of(r, s), r]
    keep_u = pltpu.make_async_copy(uout, refined_hbm, lsem.at[4])
    keep_u.start()
    for cp in started:
        cp.wait_send()
    keep_d.wait()
    keep_u.wait()


COPIES = 12 + 6 + 12


def body(correlation, factor, pattern):
    any_space = pl.BlockSpec(memory_space=pl.ANY)
    out = jax.ShapeDtypeStruct(factor.shape, F32)
    tiles = lambda *lead: pltpu.VMEM((*lead, T, T), F32)
    return pl.pallas_call(
        kernel,
        out_shape=(out, out),
        in_specs=[any_space] * 3,
        out_specs=(any_space, any_space),
        scratch_shapes=[
            pltpu.SMEM(pattern.T.shape, jnp.int32),
            tiles(2, SLOTS + 1),
            tiles(2, SLOTS + 1),
            tiles(8, 7),
            pltpu.VMEM((4 * T, 8 * T), BF16),
            *[pltpu.VMEM((8 * T, 8 * T), BF16)] * 4,
            tiles(8, 2),
            tiles(2, 8),
            pltpu.VMEM((2, 7 * T, 2 * T), BF16),
            tiles(2, 8),
            tiles(8, 2),
            pltpu.VMEM((2, 7 * T, 2 * T), BF16),
            tiles(2, 8),
            tiles(8, 2),
            tiles(2, SLOTS),
            tiles(2, SLOTS),
            pltpu.SemaphoreType.DMA((5,)),
            pltpu.SemaphoreType.DMA((COPIES,)),
            pltpu.SemaphoreType.DMA((COPIES,)),
        ],
        compiler_params=pltpu.CompilerParams(
            collective_id=0, has_side_effects=True, vmem_limit_bytes=48 << 20
        ),
    )(correlation, factor, pattern.T)


def solution(mesh):
    rows = P(("blk", "sub"), None, None, None)
    return jax.shard_map(body, mesh=mesh, in_specs=(rows, rows, P()), out_specs=(rows, rows), check_vma=False)
```

time: 196 us -> 73.6 us (0.38)
  waiting for transfers between devices: 75.6 us -> 0 us
  Pallas kernels: 0 us -> 67.8 us
  local copies, waits for them, and re-layouts: 52.2 us -> 4.86 us
  starting transfers between devices: 41.8 us -> 0 us
  matrix products: 21.5 us -> 0 us
  other arithmetic: 3.23 us -> 0 us
    ppermute x12 -> x0, waiting for transfers between devices: 75.6 us -> none  [passed_along(): lax.ppermute(value, axis, [(i, (i + by) % size) for i in range(size)])]
    pallas_call x0 -> x1, Pallas kernels: none -> 67.8 us  [body(): pl.pallas_call(kernel, out_shape=(out, out), in_specs=[any_space] * 3, ou...]
    ppermute x12 -> x0, starting transfers between devices: 41.8 us -> none  [passed_along(): lax.ppermute(value, axis, [(i, (i + by) % size) for i in range(size)])]
    dot_general x3 -> x0, matrix products: 21.5 us -> none  [the longest x1 9.35 us: body(): jnp.einsum('tqab,tpqbc->tpac', correlation, chosen, precision=lax.Precisi...]
    unnamed x23 -> x8, local copies, waits for them, and re-layouts: 25.7 us -> 4.86 us
    gather x13 -> x0, local copies, waits for them, and re-layouts: 19.7 us -> none  [the longest x4 17.5 us: select_tiles(): return window_flat[flat_index]]
    slice x3 -> x0, local copies, waits for them, and re-layouts: 3.89 us -> none  [neighbour_window(): sources = ((2, tiles[rows_here - edge_count:]), (-2, tiles[:edge_count]))]
  transfers between devices with their start and end apart: 12 -> 0, of which waited for: 5 -> 0; matrix products, arithmetic and copies ran while one was open for 17% -> 0% of each run, Pallas kernels for 0% -> 0%
where the time goes in v1:
time: 73.6 us; the launch traced here: 73.3 us
  Pallas kernels  67.8 us (92%)
  local copies, waits for them, and re-layouts  4.86 us (7%)
    pallas_call x1, Pallas kernels, body(): pl.pallas_call(kernel, out_shape=(out, out), in_specs=[any_space] * 3, ou...  67.8 us
    unnamed x8, local copies, waits for them, and re-layouts  4.86 us

profile of v1, /device:TPU:1, one launch (start us, length us, event | category | flops | bytes accessed | tf_op | source)
XLA Modules:
  0.0 73.3 jit_solution(17859289222217918469)
XLA Ops:
  0.6 0.0 copy-start
  0.6 1.1 %copy-done = f32[2,6,128,128]{3,2,1,0:T(8,128)S(1)} copy-done((f32[2,6,128,128]{3,2,1,0:T(8,128)S(1)}, f32[2,6,128,128]{3,2,1,0:T(8,128)}, u32[]{:S(2)}) %copy-start) | copy-done | bytes 786456
  1.8 0.0 copy-start.1
  1.8 1.1 %copy-done.1 = f32[2,6,128,128]{3,2,1,0:T(8,128)S(1)} copy-done((f32[2,6,128,128]{3,2,1,0:T(8,128)S(1)}, f32[2,6,128,128]{3,2,1,0:T(8,128)}, u32[]{:S(2)}) %copy-start.1) | copy-done | bytes 786456
  2.9 0.0 copy-start.2
  2.9 0.8 %copy-done.2 = s32[2048,6]{0,1:T(8,128)S(1)} copy-done((s32[2048,6]{0,1:T(8,128)S(1)}, s32[2048,6]{0,1:T(8,128)}, u32[]{:S(2)}) %copy-start.2) | copy-done | bytes 49176
  3.7 67.8 %shard_map.50 = (f32[2,6,128,128]{3,2,1,0:T(8,128)S(1)}, f32[2,6,128,128]{3,2,1,0:T(8,128)S(1)}) custom-call(f32[2,6,128,128]{3,2,1,0:T(8,128)S(1)} %copy-done, f32[2,6,128,128]{3,2,1,0:T(8,128)S(1)} %copy-done.1, s32[6,2048]{1,0:T(8,128)S(1)} %bitcast.1), custom_call_target="tpu_custom_call" | custom-call | tf_op jit(solution)/shard_map/pallas_call | solution.py:305
  71.6 0.9 %copy.7 = f32[2,6,128,128]{3,2,1,0:T(8,128)} copy(f32[2,6,128,128]{3,2,1,0:T(8,128)S(1)} %get-tuple-element.4) | data formatting | bytes 1572864
  72.5 0.9 %copy.8 = f32[2,6,128,128]{3,2,1,0:T(8,128)} copy(f32[2,6,128,128]{3,2,1,0:T(8,128)S(1)} %get-tuple-element.5) | data formatting | bytes 1572864
Async XLA Ops:
  0.6 1.1 %copy-start = (f32[2,6,128,128]{3,2,1,0:T(8,128)S(1)}, f32[2,6,128,128]{3,2,1,0:T(8,128)}, u32[]{:S(2)}) copy-start(f32[2,6,128,128]{3,2,1,0:T(8,128)} %corr_hbm.1) | copy-start | bytes 2359300
  1.8 1.1 %copy-start.1 = (f32[2,6,128,128]{3,2,1,0:T(8,128)S(1)}, f32[2,6,128,128]{3,2,1,0:T(8,128)}, u32[]{:S(2)}) copy-start(f32[2,6,128,128]{3,2,1,0:T(8,128)} %fact_hbm.1) | copy-start | bytes 2359300
  2.9 0.8 %copy-start.2 = (s32[2048,6]{0,1:T(8,128)S(1)}, s32[2048,6]{0,1:T(8,128)}, u32[]{:S(2)}) copy-start(s32[2048,6]{0,1:T(8,128)} %param.5) | copy-start | bytes 147460

commit v2 on v1

--- a/solution.py
+++ b/solution.py
@@ -6,6 +6,7 @@
 from jax.sharding import PartitionSpec as P
 
 T = 128
+RING = 32
 SLOTS = 6
 OFFS = (-3, -2, -1, 1, 2, 3)
 F32 = jnp.float32
@@ -23,14 +24,16 @@
 
 
 def kernel(
-    corr_hbm, fact_hbm, pat_hbm, refined_hbm, correction_hbm,
+    corr_hbm, fact_hbm, pat_hbm, refined, correction,
     pat, zraw, sraw, zwin, scat, zh, zl, zth, ztl, psend, pcol, pcat,
-    dsend, drow, dcat, usend, urow, dout, uout, lsem, ssem, rsem,
+    dsend, drow, dcat, usend, urow, lsem, ssem, rsem, here,
 ):
     blks, subs = lax.axis_size("blk"), lax.axis_size("sub")
     world = blks * subs
     rows_all = 2 * world
-    me = lax.axis_index("blk") * subs + lax.axis_index("sub")
+    blk, sub = lax.axis_index("blk"), lax.axis_index("sub")
+    me = blk * subs + sub
+    opens = (sub == 0) & (lax.rem(blk, RING) == 0)
 
     def device(by):
         d = lax.rem(me + by + world, world)
@@ -47,8 +50,8 @@
     load_s.start()
 
     barrier = pltpu.get_barrier_semaphore()
-    for by in (-2, -1, 1, 2):
-        pl.semaphore_signal(barrier, inc=1, device_id=device(by), device_id_type=MESH)
+    for partner in (device(-1), device(-2)):
+        pl.semaphore_signal(barrier, inc=1, device_id=partner, device_id_type=MESH)
 
     zero = jnp.zeros((T, T), F32)
     for r in range(2):
@@ -106,30 +109,42 @@
         for o in range(7):
             zwin[3 + r, o] = dense(zraw, r, o)
 
-    pl.semaphore_wait(barrier, 4)
+    pl.semaphore_wait(barrier, 2)
+    for by in (1, 2):
+        pl.semaphore_signal(here.at[by - 1], inc=1, device_id=device(by), device_id_type=MESH)
 
     count = [0]
     started = []
 
-    def send(src, dst, by):
+    def copy(src, dst, by):
         k = count[0]
         count[0] += 1
         cp = pltpu.make_async_remote_copy(
             src_ref=src, dst_ref=dst, send_sem=ssem.at[k], recv_sem=rsem.at[k],
             device_id=device(by), device_id_type=MESH,
         )
-        cp.start()
         started.append(cp)
         return cp
 
-    def send_z(row_from, row_to, o, n, by):
-        return send(zwin.at[row_from, pl.ds(o, n)], zwin.at[row_to, pl.ds(o, n)], by)
+    def send(src, dst, by):
+        cp = copy(src, dst, by)
+        cp.start()
+        return cp
+
+    def copy_z(row_from, row_to, o, n, by):
+        return copy(zwin.at[row_from, pl.ds(o, n)], zwin.at[row_to, pl.ds(o, n)], by)
+
+    def send_z(*where):
+        cp = copy_z(*where)
+        cp.start()
+        return cp
 
     r1 = send_z(4, 2, 3, 4, 1)
+    r2 = send_z(4, 2, 1, 2, 1)
+    r3 = send_z(3, 1, 2, 3, 1)
+    pl.semaphore_wait(here.at[0], 1)
     l1 = send_z(3, 5, 0, 4, -1)
-    r2 = send_z(4, 2, 1, 2, 1)
     l2 = send_z(3, 5, 4, 2, -1)
-    r3 = send_z(3, 1, 2, 3, 1)
     l3 = send_z(4, 6, 2, 3, -1)
 
     def place(w, offsets):
@@ -155,24 +170,25 @@
             scat[r * T : (r + 1) * T, c * T : (c + 1) * T] = hi
             scat[(2 + r) * T : (3 + r) * T, c * T : (c + 1) * T] = lo
 
-    r1.wait_recv()
-    f1 = send_z(2, 0, 3, 3, 1)
+    f1, r4 = copy_z(2, 0, 3, 4, 1), copy_z(3, 1, 5, 2, 1)
+    g1, l4 = copy_z(5, 7, 0, 4, -1), copy_z(4, 6, 0, 2, -1)
+
+    def pass_on():
+        r1.wait_recv()
+        f1.start()
+        r4.start()
+
+    pl.when(jnp.logical_not(opens))(pass_on)
     l1.wait_recv()
-    g1 = send_z(5, 7, 1, 3, -1)
-    r4 = send_z(3, 1, 5, 2, 1)
-    l4 = send_z(4, 6, 0, 2, -1)
-    f2 = send_z(2, 0, 6, 1, 1)
-    g2 = send_z(5, 7, 0, 1, -1)
-    place(2, range(3, 7))
+    g1.start()
+    l4.start()
     place(5, range(4))
-    r2.wait_recv()
-    place(2, range(1, 3))
     l2.wait_recv()
     place(5, range(4, 6))
-    r3.wait_recv()
-    place(1, range(2, 5))
     l3.wait_recv()
     place(6, range(2, 5))
+    g1.wait_recv()
+    place(7, range(4))
 
     def product(rows, columns):
         k, n = slice(rows[0] * T, rows[1] * T), slice(columns[0] * T, columns[1] * T)
@@ -185,27 +201,31 @@
                 tile = x[r * T : (r + 1) * T, n * T : (n + 1) * T]
                 ref[index(first + n, r)] = masked(tile, 3 + r, first + n)
 
+    def by_column(c, r):
+        return (c, r)
+
+    keep_product(product((3, 8), (6, 8)), 6, psend, by_column)
+    pr2 = send(psend.at[6], pcol.at[1, pl.ds(1, 2)], 1)
+    pr0 = send(psend.at[7, pl.ds(1, 1)], pcol.at[0, pl.ds(0, 1)], 2)
+    pl.when(opens)(pass_on)
+    place(2, range(3, 7))
+    keep_product(product((2, 8), (5, 6)), 5, psend, by_column)
+    pr1 = send(psend.at[5], pcol.at[0, pl.ds(1, 2)], 1)
+    r2.wait_recv()
+    place(2, range(1, 3))
+    r3.wait_recv()
+    place(1, range(2, 5))
     f1.wait_recv()
-    place(0, range(3, 6))
-    keep_product(product((0, 6), (0, 3)), 0, psend, lambda c, r: (c, r))
+    place(0, range(3, 7))
+    keep_product(product((0, 6), (0, 3)), 0, psend, by_column)
+    pl.semaphore_wait(here.at[1], 1)
+    pl0 = send(psend.at[0, pl.ds(0, 1)], pcol.at[1, pl.ds(7, 1)], -2)
+    pl2 = send(psend.at[2], pcol.at[1, pl.ds(5, 2)], -1)
     pl1 = send(psend.at[1], pcol.at[0, pl.ds(5, 2)], -1)
-    g1.wait_recv()
-    place(7, range(1, 4))
-    keep_product(product((2, 8), (5, 8)), 5, psend, lambda c, r: (c, r))
-    pr0 = send(psend.at[7, pl.ds(1, 1)], pcol.at[0, pl.ds(0, 1)], 2)
-    pr1 = send(psend.at[5], pcol.at[0, pl.ds(1, 2)], 1)
-    pl0 = send(psend.at[0, pl.ds(0, 1)], pcol.at[1, pl.ds(7, 1)], -2)
-    pr2 = send(psend.at[6], pcol.at[1, pl.ds(1, 2)], 1)
-    pl2 = send(psend.at[2], pcol.at[1, pl.ds(5, 2)], -1)
-
     r4.wait_recv()
     place(1, range(5, 7))
     l4.wait_recv()
     place(6, range(2))
-    f2.wait_recv()
-    place(0, (6,))
-    g2.wait_recv()
-    place(7, (0,))
     keep_product(product((0, 8), (3, 5)), 3, pcol, lambda c, r: (c - 3, 3 + r))
 
     identity = (
@@ -256,18 +276,18 @@
             if w in (3, 4):
                 urow[3 + c, w - 3] = tile
 
-    for cp in (pl1, pr0, pr1):
+    for cp in (pl0, pl2, pr2):
+        cp.wait_recv()
+    gram(1)
+    dcps = send_column(dsend, drow, 1)
+    for cp in (pr0, pr1, pl1):
         cp.wait_recv()
     gram(0)
-    dcps = send_column(dsend, drow, 0)
-    for cp in (pl0, pr2, pl2):
-        cp.wait_recv()
-    gram(1)
-    dcps += send_column(dsend, drow, 1)
+    dcps += send_column(dsend, drow, 0)
+    update(1)
+    ucps = send_column(usend, urow, 1)
     update(0)
-    ucps = send_column(usend, urow, 0)
-    update(1)
-    ucps += send_column(usend, urow, 1)
+    ucps += send_column(usend, urow, 0)
 
     def column_of(r, s):
         if s == 0:
@@ -279,34 +299,28 @@
         cp.wait_recv()
     for r in range(2):
         for s in range(SLOTS):
-            dout[r, s] = drow[column_of(r, s), r]
-    keep_d = pltpu.make_async_copy(dout, correction_hbm, lsem.at[3])
-    keep_d.start()
+            correction[r, s] = drow[column_of(r, s), r]
     for cp in ucps:
         cp.wait_recv()
     for r in range(2):
         for s in range(SLOTS):
-            uout[r, s] = zraw[r, s] + 0.5 * urow[column_of(r, s), r]
-    keep_u = pltpu.make_async_copy(uout, refined_hbm, lsem.at[4])
-    keep_u.start()
+            refined[r, s] = zraw[r, s] + 0.5 * urow[column_of(r, s), r]
     for cp in started:
         cp.wait_send()
-    keep_d.wait()
-    keep_u.wait()
-
-
-COPIES = 12 + 6 + 12
+
+
+COPIES = 10 + 6 + 12
 
 
 def body(correlation, factor, pattern):
-    any_space = pl.BlockSpec(memory_space=pl.ANY)
-    out = jax.ShapeDtypeStruct(factor.shape, F32)
+    hbm_space = pl.BlockSpec(memory_space=pltpu.HBM)
+    out = pltpu.VMEM(factor.shape, F32)
     tiles = lambda *lead: pltpu.VMEM((*lead, T, T), F32)
     return pl.pallas_call(
         kernel,
         out_shape=(out, out),
-        in_specs=[any_space] * 3,
-        out_specs=(any_space, any_space),
+        in_specs=[hbm_space] * 3,
+        out_specs=(pl.BlockSpec(memory_space=pltpu.VMEM),) * 2,
         scratch_shapes=[
             pltpu.SMEM(pattern.T.shape, jnp.int32),
             tiles(2, SLOTS + 1),
@@ -322,14 +336,13 @@
             pltpu.VMEM((2, 7 * T, 2 * T), BF16),
             tiles(2, 8),
             tiles(8, 2),
-            tiles(2, SLOTS),
-            tiles(2, SLOTS),
-            pltpu.SemaphoreType.DMA((5,)),
+            pltpu.SemaphoreType.DMA((3,)),
             pltpu.SemaphoreType.DMA((COPIES,)),
             pltpu.SemaphoreType.DMA((COPIES,)),
+            pltpu.SemaphoreType.REGULAR((2,)),
         ],
         compiler_params=pltpu.CompilerParams(
-            collective_id=0, has_side_effects=True, vmem_limit_bytes=48 << 20
+            collective_id=0, has_side_effects=True, vmem_limit_bytes=60 << 20
         ),
     )(correlation, factor, pattern.T)
 

time: 73.6 us -> 65 us (0.88)
  Pallas kernels: 67.8 us -> 62.4 us
  local copies, waits for them, and re-layouts: 4.86 us -> 1.76 us
    pallas_call x1, Pallas kernels: 67.8 us -> 62.4 us  [body(): pl.pallas_call(kernel, out_shape=(out, out), in_specs=[hbm_space] * 3, ou...]
    unnamed x8 -> x2, local copies, waits for them, and re-layouts: 4.86 us -> 1.76 us
where the time goes in v2:
time: 65 us; the launch traced here: 64.8 us
  Pallas kernels  62.4 us (96%)
  local copies, waits for them, and re-layouts  1.76 us (3%)
    pallas_call x1, Pallas kernels, body(): pl.pallas_call(kernel, out_shape=(out, out), in_specs=[hbm_space] * 3, ou...  62.4 us
    unnamed x2, local copies, waits for them, and re-layouts  1.76 us

profile of v2, /device:TPU:1, one launch (start us, length us, event | category | flops | bytes accessed | tf_op | source)
XLA Modules:
  0.0 64.8 jit_solution(10875727457922613659)
XLA Ops:
  0.6 62.4 %shard_map.50 = (f32[2,6,128,128]{3,2,1,0:T(8,128)S(1)}, f32[2,6,128,128]{3,2,1,0:T(8,128)S(1)}) custom-call(f32[2,6,128,128]{3,2,1,0:T(8,128)} %corr_hbm.1, f32[2,6,128,128]{3,2,1,0:T(8,128)} %fact_hbm.1, s32[6,2048]{1,0:T(8,128)} %bitcast.1), custom_call_target="tpu_custom_call" | custom-call | tf_op jit(solution)/shard_map/pallas_call | solution.py:319
  63.0 0.9 %copy.7 = f32[2,6,128,128]{3,2,1,0:T(8,128)} copy(f32[2,6,128,128]{3,2,1,0:T(8,128)S(1)} %get-tuple-element.2) | data formatting | bytes 1572864
  63.9 0.9 %copy.8 = f32[2,6,128,128]{3,2,1,0:T(8,128)} copy(f32[2,6,128,128]{3,2,1,0:T(8,128)S(1)} %get-tuple-element.3) | data formatting | bytes 1572864

commit v3 on v2

--- a/solution.py
+++ b/solution.py
@@ -309,6 +309,18 @@
         cp.wait_send()
 
 
+def store(refined, correction, refined_hbm, correction_hbm, sem):
+    copies = [
+        pltpu.make_async_copy(src.at[r], dst.at[r], sem.at[2 * n + r])
+        for n, (src, dst) in enumerate(((refined, refined_hbm), (correction, correction_hbm)))
+        for r in range(2)
+    ]
+    for cp in copies:
+        cp.start()
+    for cp in copies:
+        cp.wait()
+
+
 COPIES = 10 + 6 + 12
 
 
@@ -316,7 +328,7 @@
     hbm_space = pl.BlockSpec(memory_space=pltpu.HBM)
     out = pltpu.VMEM(factor.shape, F32)
     tiles = lambda *lead: pltpu.VMEM((*lead, T, T), F32)
-    return pl.pallas_call(
+    done = pl.pallas_call(
         kernel,
         out_shape=(out, out),
         in_specs=[hbm_space] * 3,
@@ -345,6 +357,14 @@
             collective_id=0, has_side_effects=True, vmem_limit_bytes=60 << 20
         ),
     )(correlation, factor, pattern.T)
+    return pl.pallas_call(
+        store,
+        out_shape=(pltpu.HBM(factor.shape, F32),) * 2,
+        in_specs=[pl.BlockSpec(memory_space=pl.ANY)] * 2,
+        out_specs=(pl.BlockSpec(memory_space=pltpu.HBM),) * 2,
+        scratch_shapes=[pltpu.SemaphoreType.DMA((4,))],
+        compiler_params=pltpu.CompilerParams(vmem_limit_bytes=4 << 20),
+    )(*done)
 
 
 def solution(mesh):

time: 65 us -> 64.4 us (level)
  local copies, waits for them, and re-layouts: 1.76 us -> 0 us
  Pallas kernels: 62.4 us -> 63.6 us
    unnamed x2 -> x0, local copies, waits for them, and re-layouts: 1.76 us -> none
    pallas_call x0 -> x1, Pallas kernels: none -> 1.17 us  [body(): pl.pallas_call(store, out_shape=(pltpu.HBM(factor.shape, F32),) * 2, in_s...]
where the time goes in v3:
time: 64.4 us; the launch traced here: 64.2 us
  Pallas kernels  63.6 us (99%)
    pallas_call x1, Pallas kernels, body(): pl.pallas_call(kernel, out_shape=(out, out), in_specs=[hbm_space] * 3, ou...  62.4 us

profile of v3, /device:TPU:1, one launch (start us, length us, event | category | flops | bytes accessed | tf_op | source)
XLA Modules:
  0.0 64.2 jit_solution(6408535402361893778)
XLA Ops:
  0.6 62.4 %shard_map.50 = (f32[2,6,128,128]{3,2,1,0:T(8,128)S(1)}, f32[2,6,128,128]{3,2,1,0:T(8,128)S(1)}) custom-call(f32[2,6,128,128]{3,2,1,0:T(8,128)} %corr_hbm.1, f32[2,6,128,128]{3,2,1,0:T(8,128)} %fact_hbm.1, s32[6,2048]{1,0:T(8,128)} %bitcast.1), custom_call_target="tpu_custom_call" | custom-call | tf_op jit(solution)/shard_map/pallas_call | solution.py:331
  63.0 1.2 %shard_map.51 = (f32[2,6,128,128]{3,2,1,0:T(8,128)}, f32[2,6,128,128]{3,2,1,0:T(8,128)}) custom-call(f32[2,6,128,128]{3,2,1,0:T(8,128)S(1)} %get-tuple-element.4.refined, f32[2,6,128,128]{3,2,1,0:T(8,128)S(1)} %get-tuple-element.5.correction), custom_call_target="tpu_custom_call" | custom-call | tf_op jit(solution)/shard_map/pallas_call | solution.py:360

commit v4 on v3

--- a/solution.py
+++ b/solution.py
@@ -176,9 +176,9 @@
     def pass_on():
         r1.wait_recv()
         f1.start()
-        r4.start()
 
     pl.when(jnp.logical_not(opens))(pass_on)
+    r4.start()
     l1.wait_recv()
     g1.start()
     l4.start()

time: 64.4 us -> 64.4 us (level)
  no operation moved by 1% of the time
where the time goes in v4:
time: 64.4 us; the launch traced here: 64.2 us
  Pallas kernels  63.6 us (99%)
    pallas_call x1, Pallas kernels, body(): pl.pallas_call(kernel, out_shape=(out, out), in_specs=[hbm_space] * 3, ou...  62.4 us

profile of v4, /device:TPU:1, one launch (start us, length us, event | category | flops | bytes accessed | tf_op | source)
XLA Modules:
  0.0 64.2 jit_solution(16997930803485644941)
XLA Ops:
  0.6 62.4 %shard_map.50 = (f32[2,6,128,128]{3,2,1,0:T(8,128)S(1)}, f32[2,6,128,128]{3,2,1,0:T(8,128)S(1)}) custom-call(f32[2,6,128,128]{3,2,1,0:T(8,128)} %corr_hbm.1, f32[2,6,128,128]{3,2,1,0:T(8,128)} %fact_hbm.1, s32[6,2048]{1,0:T(8,128)} %bitcast.1), custom_call_target="tpu_custom_call" | custom-call | tf_op jit(solution)/shard_map/pallas_call | solution.py:331
  63.0 1.2 %shard_map.51 = (f32[2,6,128,128]{3,2,1,0:T(8,128)}, f32[2,6,128,128]{3,2,1,0:T(8,128)}) custom-call(f32[2,6,128,128]{3,2,1,0:T(8,128)S(1)} %get-tuple-element.4.refined, f32[2,6,128,128]{3,2,1,0:T(8,128)S(1)} %get-tuple-element.5.correction), custom_call_target="tpu_custom_call" | custom-call | tf_op jit(solution)/shard_map/pallas_call | solution.py:360
